TPU v7x, 512 devices: a whole 4x4x16 slice. The times are simulated.
512 devices in a mesh: rx: 32 (over z_lo, x), tx: 16 (over y, z_hi, core).
Axes of the slice: x: 4, y: 4, z: 16 (z_hi: 2, z_lo: 8; z = z_hi * 8 + z_lo), core: 2. Of those that a mesh axis runs over, the one named last changes fastest.
Arguments:
- sender_xy: int32 [2, 32768], P(None, ('tx', 'rx')), may hold values from 0 to 255, as said below
- listener_xy: int32 [2, 32768], P(None, ('rx', 'tx')), may hold values from 0 to 256, as said below
- powers: float32 [32768, 128], P(('tx', 'rx')), may hold values from 0.25 to 1
- weight: int32 [32768], P(('rx', 'tx')), may hold values from 1 to 16
- fairness: int32 [32768], P(('rx', 'tx')), may hold values from 0 to 2
- step_code: int32 [1], replicated, may hold values from 256 to 4096
Outputs:
- quality: float32 [32768, 128], P(('rx', 'tx'))
- gradient: float32 [32768, 128], P(('tx', 'rx'))
- new_power: float32 [32768, 128], P(('tx', 'rx'))
- duality_gap: float32 [1], replicated
Inputs may be any that keep to these rules, and one draw needn't show every extreme that they name: `sender_xy`: row 0 lies in 0 to 255 and row 1 in 0 to 255. `listener_xy`: each entry equals the sender_xy entry of the same user or exceeds it by one.
All inputs are finite; a program needn't handle non-finite values.
Results may differ from a plain program's by a relative error of at most 0.0003.
Values sent between devices are 32-bit elements; how exact they have to be, the bound alone decides.
No kernel may reach another device: no remote copies, remote signals or barrier semaphores. Data moves between devices by JAX's collectives and lax.ppermute only.
A program may use at most 64 MiB of HBM per device.

v0:
```python
import jax
import jax.numpy as jnp
from jax import lax
from jax.sharding import PartitionSpec as P

NOISE_POWER = 0.05
ARRAY_GAIN = 32.0
WEIGHT_UNIT = 1.0 / 16.0
PEAK_POWER = 1.0


def path_gain(listen, sender):
    delta_x = listen[0].astype(jnp.float32)[:, None] - sender[0].astype(jnp.float32)[None, :]
    delta_y = listen[1].astype(jnp.float32)[:, None] - sender[1].astype(jnp.float32)[None, :]
    return 1.0 / (1.0 + delta_x * delta_x + delta_y * delta_y)


def derivatives(interference, signal, user_weight, user_fair):
    denominator = NOISE_POWER + interference
    quality = signal / denominator
    user_scale = WEIGHT_UNIT * user_weight.astype(jnp.float32)
    marginal = (
        user_scale[:, None]
        * jnp.exp(-user_fair.astype(jnp.float32)[:, None] * jnp.log(quality))
        / denominator
    )
    return (quality, marginal, marginal * quality)


def per_device(sender_xy, listener_xy, powers, weight, fairness, step_code):
    rx_here = lax.axis_index("rx")
    tx_here = lax.axis_index("tx")
    user_rows = powers.shape[0]
    channels = powers.shape[1]
    senders, sender_power = (
        lax.all_gather(sender_xy, "rx", axis=1, tiled=True),
        lax.all_gather(powers, "rx", axis=0, tiled=True),
    )
    listeners = lax.all_gather(listener_xy, "tx", axis=1, tiled=True)
    rx_width = listeners.shape[1]
    tx_width = senders.shape[1]
    row_start = rx_here * rx_width
    col_start = tx_here * tx_width
    gain_tile = path_gain(listeners, senders)
    row_ids = row_start + jnp.arange(rx_width, dtype=jnp.int32)
    col_ids = col_start + jnp.arange(tx_width, dtype=jnp.int32)
    diagonal = row_ids[:, None] == col_ids[None, :]
    crossing = jnp.where(diagonal, 0.0, gain_tile)
    own_gain = jnp.sum(jnp.where(diagonal, gain_tile, 0.0), axis=1)
    offset = row_start % tx_width
    interference_part = jnp.dot(crossing, sender_power, precision=lax.Precision.HIGHEST)
    signal_part = (
        ARRAY_GAIN * own_gain[:, None] * lax.dynamic_slice_in_dim(sender_power, offset, rx_width, 0)
    )
    interference, signal = (
        lax.psum_scatter(interference_part, "tx", scatter_dimension=0, tiled=True),
        lax.psum_scatter(signal_part, "tx", scatter_dimension=0, tiled=True),
    )
    quality, marginal, pressure = derivatives(interference, signal, weight, fairness)
    marginal_all, pressure_all = (
        lax.all_gather(marginal, "tx", axis=0, tiled=True),
        lax.all_gather(pressure, "tx", axis=0, tiled=True),
    )
    own_term = ARRAY_GAIN * own_gain[:, None] * marginal_all
    own_full = lax.dynamic_update_slice_in_dim(
        jnp.zeros((tx_width, channels), jnp.float32), own_term, offset, 0
    )
    pushed = lax.dot_general(
        crossing, pressure_all, (((0,), (0,)), ((), ())), precision=lax.Precision.HIGHEST
    )
    totals = lax.psum(own_full - pushed, "rx")
    gradient = lax.dynamic_slice_in_dim(totals, rx_here * user_rows, user_rows, 0)
    target = PEAK_POWER * jax.nn.sigmoid(gradient)
    step_size = step_code[0].astype(jnp.float32) / 4096.0
    new_power = powers + step_size * (target - powers)
    gap_local = jnp.sum(PEAK_POWER * jnp.maximum(gradient, 0.0) - gradient * powers)
    gap_sum = lax.psum(gap_local, ("rx", "tx"))
    duality_gap = (
        gap_sum / (user_rows * channels * lax.axis_size("rx") * lax.axis_size("tx"))
    ).reshape(1)
    return (quality, gradient, new_power, duality_gap)


def solution(mesh):
    placed = (
        P(None, ("tx", "rx")),
        P(None, ("rx", "tx")),
        P(("tx", "rx"), None),
        P(("rx", "tx")),
        P(("rx", "tx")),
        P(),
    )
    return jax.shard_map(
        per_device,
        mesh=mesh,
        in_specs=placed,
        out_specs=(P(("rx", "tx"), None), P(("tx", "rx"), None), P(("tx", "rx"), None), P()),
        check_vma=False,
    )
```

profile of v0, /device:TPU:1, one launch (start us, length us, event | category | flops | bytes accessed | tf_op | source)
XLA Modules:
  0.0 1118.0 jit_solution(16016938262697707755)
XLA Ops:
  7.2 0.0 all-gather.4.cloned.1.call-start
  7.2 0.7 all-gather.4.cloned.1.call-update
  7.9 0.0 reduce-scatter.3.cloned.1.call-start
  8.0 51.2 %all-gather = s32[16,64,2]{1,2,0:T(2,128)S(1)} all-gather(s32[1,64,2]{1,2,0:T(2,128)} %bitcast.34), channel_id=1, replica_groups=mesh['rx'=32,'tx'=16] {'tx'}, dimensions={0}, use_global_device_ids=true | all-gather | bytes 8704 | tf_op jit(solution)/shard_map/all_gather | solution.py:39
  59.1 0.1 reshape.43
  59.3 104.0 %all-gather.1 = s32[32,64,2]{1,2,0:T(2,128)S(1)} all-gather(s32[1,64,2]{1,2,0:T(2,128)} %bitcast.35), channel_id=1, replica_groups=mesh['rx'=32,'tx'=16] {'rx'}, dimensions={0}, use_global_device_ids=true | all-gather | bytes 16896 | tf_op jit(solution)/shard_map/all_gather | solution.py:36
  163.3 0.1 reshape.45
  163.5 3.1 fusion
  166.5 49.7 %all-gather.4.cloned.1.call-done = f32[2048,128]{1,0:T(8,128)} async-done(((f32[64,128]{1,0:T(8,128)}), f32[2048,128]{1,0:T(8,128)}) %all-gather.4.cloned.1.call-update) | async-done | bytes 1048592 | tf_op jit(solution)/shard_map/all_gather | solution.py:37
  216.2 0.0 copy-start.1
  216.2 2.1 dynamic-slice_multiply_fusion
  218.4 0.0 reduce-scatter.3.cloned.1.call-update
  218.4 0.0 copy-start.3
  218.4 0.0 copy-start.4
  218.4 0.0 reduce-scatter.5.cloned.1.call-start
  218.5 0.0 copy-done.1
  218.5 9.3 fusion.2
  227.8 0.0 reduce-scatter.5.cloned.1.call-update
  227.8 0.0 all-reduce.2.cloned.1.call-start
  227.9 0.0 copy-done.3
  227.9 0.0 copy-done.4
  227.9 111.3 %reduce-scatter.3.cloned.1.call-done = f32[64,128]{1,0:T(8,128)} async-done(((f32[1024,128]{1,0:T(8,128)}), f32[64,128]{1,0:T(8,128)}) %reduce-scatter.3.cloned.1.call-update) | async-done | bytes 32784 | tf_op jit(solution)/shard_map/reduce_scatter | solution.py:57
  339.2 96.6 %reduce-scatter.5.cloned.1.call-done = f32[64,128]{1,0:T(8,128)} async-done(((f32[1024,128]{1,0:T(8,128)}), f32[64,128]{1,0:T(8,128)}) %reduce-scatter.5.cloned.1.call-update) | async-done | bytes 32784 | tf_op jit(solution)/shard_map/reduce_scatter | solution.py:56
  435.8 1.4 fusion.14
  437.2 43.2 %all_gather.18 = f32[1024,128]{1,0:T(8,128)S(1)} all-gather(f32[64,128]{1,0:T(8,128)S(1)} %get-tuple-element.7), channel_id=1, replica_groups=mesh['rx'=32,'tx'=16] {'tx'}, dimensions={0}, use_global_device_ids=true | all-gather | bytes 557056 | tf_op jit(solution)/shard_map/all_gather | solution.py:61
  480.4 49.4 %all_gather.19 = f32[1024,128]{1,0:T(8,128)S(1)} all-gather(f32[64,128]{1,0:T(8,128)S(1)} %get-tuple-element.6), channel_id=1, replica_groups=mesh['rx'=32,'tx'=16] {'tx'}, dimensions={0}, use_global_device_ids=true | all-gather | bytes 557056 | tf_op jit(solution)/shard_map/all_gather | solution.py:62
  529.7 0.1 broadcast_in_dim.7
  529.8 0.2 multiply_dynamic-update-slice_fusion
  530.0 16.3 %fusion.9 = f32[2048,128]{1,0:T(8,128)} fusion(f32[2048,128]{1,0:T(8,128)S(1)} %multiply_dynamic-update-slice_fusion, f32[1024,128]{1,0:T(8,128)S(1)} %all_gather.19, f32[2048]{0:T(1024)S(1)} %bitcast.27, f32[1024]{0:T(1024)S(1)} %bitcast.33, f32[2048]{0:T(1024)S(1)} %bitcast.24, f32[1024]{0:T(1024)S(1)} %bitcast.30, s32[2048]{0:T(1024)S(1)} %iota_add_fusion, ...), kind=kOutput, calls=%fused_computation.12 | convolution fusion | flops 3240361984 | bytes 2658304 | tf_op jit(solution)/shard_map/dot_general | solution.py:68
  546.3 0.0 copy-start
  546.3 0.0 all-reduce.2.cloned.1.call-update
  547.0 437.2 %all-reduce.2.cloned.1.call-done = f32[2048,128]{1,0:T(8,128)} async-done(((f32[2048,128]{1,0:T(8,128)}), f32[2048,128]{1,0:T(8,128)}) %all-reduce.2.cloned.1.call-update) | async-done | bytes 1048592 | tf_op jit(solution)/shard_map/psum | solution.py:71
  984.1 0.0 copy-done
  984.1 1.4 subtract_reduce_fusion
  985.5 0.0 copy-start.2
  985.5 123.6 %psum.15 = f32[]{:T(128)} all-reduce(f32[]{:T(128)} %get-tuple-element.4), channel_id=1, replica_groups=mesh['rx'=32,'tx'=16] {'rx','tx'}, use_global_device_ids=true, to_apply=%region_5.6 | all-reduce | flops 1 | bytes 8 | tf_op jit(solution)/shard_map/psum | solution.py:77
  1109.1 0.6 multiply_add_fusion
  1110.4 0.0 copy-done.2
  (8 shorter events, 0.0 us)
Async XLA Ops:
  7.2 209.1 %all-gather.4.cloned.1.call-start = ((), (), s32[]{:S(2)}) async-start(), calls=%async_computation.2 | async-start | bytes 1081344 | tf_op jit(solution)/shard_map/all_gather | solution.py:37
  7.9 331.3 %reduce-scatter.3.cloned.1.call-start = ((), (), s32[]{:S(2)}) async-start(), calls=%async_computation.3 | async-start | bytes 557056 | tf_op jit(solution)/shard_map/reduce_scatter | solution.py:57
  216.2 2.2 copy-start.1
  218.4 9.5 copy-start.3
  218.4 9.5 copy-start.4
  218.4 217.4 %reduce-scatter.5.cloned.1.call-start = ((), (), s32[]{:S(2)}) async-start(), calls=%async_computation.4 | async-start | bytes 557056 | tf_op jit(solution)/shard_map/reduce_scatter | solution.py:56
  227.8 756.3 %all-reduce.2.cloned.1.call-start = ((), (), s32[]{:S(2)}) async-start(), calls=%async_computation.5 | async-start | bytes 2097152 | tf_op jit(solution)/shard_map/psum | solution.py:71
  546.3 437.8 %copy-start = (f32[64,128]{1,0:T(8,128)S(1)}, f32[64,128]{1,0:T(8,128)}, u32[]{:S(2)}) copy-start(f32[64,128]{1,0:T(8,128)} %param.8) | copy-start | bytes 98308
  985.5 124.9 %copy-start.2 = (f32[64,128]{1,0:T(8,128)}, f32[64,128]{1,0:T(8,128)S(1)}, u32[]{:S(2)}) copy-start(f32[64,128]{1,0:T(8,128)S(1)} %get-tuple-element.5) | copy-start | bytes 98308
Sparse Core Ops, SparseCore 0:
  10.1 206.1 all-gather.3
  220.9 118.3 reduce-scatter.2
  344.6 91.1 reduce-scatter.4
  546.4 437.6 all-reduce.1
where the time goes:
time: 1120 us
  waiting for transfers between devices  695 us (62%)
  blocking collectives  371 us (33%)
  matrix products  25.6 us (2%)
  between operations  16.3 us (1%)
    psum x1, waiting for transfers between devices, per_device(): totals = lax.psum(own_full - pushed, 'rx')  437 us
    psum x1, blocking collectives, per_device(): gap_sum = lax.psum(gap_local, ('rx', 'tx'))  124 us
    reduce_scatter x1, waiting for transfers between devices, per_device(): lax.psum_scatter(signal_part, 'tx', scatter_dimension=0, tiled=True)  111 us
    all_gather x1, blocking collectives, per_device(): lax.all_gather(sender_xy, 'rx', axis=1, tiled=True)  104 us
    reduce_scatter x1, waiting for transfers between devices, per_device(): lax.psum_scatter(interference_part, 'tx', scatter_dimension=0, tiled=True)  96.6 us
    all_gather x1, blocking collectives, per_device(): listeners = lax.all_gather(listener_xy, 'tx', axis=1, tiled=True)  51.2 us
    all_gather x1, waiting for transfers between devices, per_device(): lax.all_gather(powers, 'rx', axis=0, tiled=True)  49.7 us
    all_gather x1, blocking collectives, per_device(): lax.all_gather(pressure, 'tx', axis=0, tiled=True)  49.4 us
  transfers between devices with their start and end apart: 4, of which 4 were waited for; matrix products, arithmetic and copies ran while one was open for 1% of the time, Pallas kernels for 0%

commit v1 on v0

--- a/solution.py
+++ b/solution.py
@@ -28,6 +28,11 @@
 
 
 def per_device(sender_xy, listener_xy, powers, weight, fairness, step_code):
+
+    def run_members_all(local_x, row_axis):
+        current_block = jax.lax.all_gather(local_x, row_axis)
+        return jnp.sum(current_block, axis=0)
+
     rx_here = lax.axis_index("rx")
     tx_here = lax.axis_index("tx")
     user_rows = powers.shape[0]
@@ -68,7 +73,7 @@
     pushed = lax.dot_general(
         crossing, pressure_all, (((0,), (0,)), ((), ())), precision=lax.Precision.HIGHEST
     )
-    totals = lax.psum(own_full - pushed, "rx")
+    totals = run_members_all(own_full - pushed, row_axis="rx")
     gradient = lax.dynamic_slice_in_dim(totals, rx_here * user_rows, user_rows, 0)
     target = PEAK_POWER * jax.nn.sigmoid(gradient)
     step_size = step_code[0].astype(jnp.float32) / 4096.0

time: 1120 us -> 1060 us (0.946)
  waiting for transfers between devices: 695 us -> 618 us
    psum x1 -> x0, waiting for transfers between devices: 437 us -> none  [per_device(): totals = lax.psum(own_full - pushed, 'rx')]
    all_gather x0 -> x1, waiting for transfers between devices: none -> 367 us  [run_members_all(): current_block = jax.lax.all_gather(local_x, row_axis)]
    psum x1, blocking collectives: 124 us -> 101 us  [per_device(): gap_sum = lax.psum(gap_local, ('rx', 'tx'))]
    reduce_scatter x1, waiting for transfers between devices: 96.6 us -> 114 us  [per_device(): lax.psum_scatter(interference_part, 'tx', scatter_dimension=0, tiled=True)]
    all_gather x1, blocking collectives: 49.4 us -> 64.4 us  [per_device(): lax.all_gather(pressure, 'tx', axis=0, tiled=True)]
    reduce_scatter x1, waiting for transfers between devices: 111 us -> 96.6 us  [per_device(): lax.psum_scatter(signal_part, 'tx', scatter_dimension=0, tiled=True)]
    reduce_sum x0 -> x1, other arithmetic: none -> 11.7 us  [run_members_all(): return jnp.sum(current_block, axis=0)]
  transfers between devices with their start and end apart: 4 -> 4, of which waited for: 4 -> 4; matrix products, arithmetic and copies ran while one was open for 1% -> 0% of each run, Pallas kernels for 0% -> 0%
where the time goes in v1:
time: 1060 us
  waiting for transfers between devices  618 us (58%)
  blocking collectives  377 us (36%)
  matrix products  26.9 us (3%)
  other arithmetic  18.7 us (2%)
  between operations  16.3 us (2%)
    all_gather x1, waiting for transfers between devices, run_members_all(): current_block = jax.lax.all_gather(local_x, row_axis)  367 us
    reduce_scatter x1, waiting for transfers between devices, per_device(): lax.psum_scatter(interference_part, 'tx', scatter_dimension=0, tiled=True)  114 us
    all_gather x1, blocking collectives, per_device(): lax.all_gather(sender_xy, 'rx', axis=1, tiled=True)  112 us
    psum x1, blocking collectives, per_device(): gap_sum = lax.psum(gap_local, ('rx', 'tx'))  101 us
    reduce_scatter x1, waiting for transfers between devices, per_device(): lax.psum_scatter(signal_part, 'tx', scatter_dimension=0, tiled=True)  96.6 us
    all_gather x1, blocking collectives, per_device(): lax.all_gather(pressure, 'tx', axis=0, tiled=True)  64.4 us
    all_gather x1, blocking collectives, per_device(): listeners = lax.all_gather(listener_xy, 'tx', axis=1, tiled=True)  56.4 us
    all_gather x1, blocking collectives, per_device(): lax.all_gather(marginal, 'tx', axis=0, tiled=True)  42.6 us
  transfers between devices with their start and end apart: 4, of which 4 were waited for; matrix products, arithmetic and copies ran while one was open for 0% of the time, Pallas kernels for 0%

profile of v1, /device:TPU:1, one launch (start us, length us, event | category | flops | bytes accessed | tf_op | source)
XLA Modules:
  0.0 1057.1 jit_solution(4130639457008122297)
XLA Ops:
  7.2 0.0 all-gather.6.cloned.1.call-start
  7.2 0.7 all-gather.6.cloned.1.call-update
  7.9 0.0 reduce-scatter.5.cloned.1.call-start
  7.9 112.2 %all-gather.2 = s32[32,64,2]{1,2,0:T(2,128)S(1)} all-gather(s32[1,64,2]{1,2,0:T(2,128)} %bitcast.36), channel_id=1, replica_groups=mesh['rx'=32,'tx'=16] {'rx'}, dimensions={0}, use_global_device_ids=true | all-gather | bytes 16896 | tf_op jit(solution)/shard_map/all_gather | solution.py:41
  120.2 0.1 reshape.46
  120.3 56.4 %all-gather.1 = s32[16,64,2]{1,2,0:T(2,128)S(1)} all-gather(s32[1,64,2]{1,2,0:T(2,128)} %bitcast.37), channel_id=1, replica_groups=mesh['rx'=32,'tx'=16] {'tx'}, dimensions={0}, use_global_device_ids=true | all-gather | bytes 8704 | tf_op jit(solution)/shard_map/all_gather | solution.py:44
  176.7 0.1 reshape.44
  176.8 39.9 %all-gather.6.cloned.1.call-done = f32[2048,128]{1,0:T(8,128)} async-done(((f32[64,128]{1,0:T(8,128)}), f32[2048,128]{1,0:T(8,128)}) %all-gather.6.cloned.1.call-update) | async-done | bytes 1048592 | tf_op jit(solution)/shard_map/all_gather | solution.py:42
  216.7 0.0 copy-start.1
  216.7 0.0 copy-start.3
  216.7 0.0 copy-start.4
  216.7 10.6 %fusion.2 = f32[1024,128]{1,0:T(8,128)} fusion(f32[2048,128]{1,0:T(8,128)} %all-gather.6.cloned.1.call-done, f32[2048]{0:T(1024)S(1)} %bitcast.27, f32[1024]{0:T(1024)S(1)} %bitcast.33, f32[2048]{0:T(1024)S(1)} %bitcast.24, f32[1024]{0:T(1024)S(1)} %bitcast.30, s32[2048]{0:T(1024)S(1)} %iota_add_fusion, s32[1024]{0:T(1024)S(1)} %iota_add_fusion.1), kind=kOutput, calls=%fused_computation.5 | convolution fusion | flops 3240099840 | bytes 1609728 | tf_op jit(solution)/shard_map/dot_general | solution.py:56
  227.4 0.0 reduce-scatter.5.cloned.1.call-update
  227.4 0.0 reduce-scatter.3.cloned.1.call-start
  227.5 3.1 fusion
  230.6 0.0 copy-done.1
  230.6 1.0 dynamic-slice_multiply_fusion
  231.6 0.0 reduce-scatter.3.cloned.1.call-update
  231.6 0.0 all-gather.8.cloned.1.call-start
  231.7 0.0 copy-done.3
  231.7 0.0 copy-done.4
  231.7 113.7 %reduce-scatter.5.cloned.1.call-done = f32[64,128]{1,0:T(8,128)} async-done(((f32[1024,128]{1,0:T(8,128)}), f32[64,128]{1,0:T(8,128)}) %reduce-scatter.5.cloned.1.call-update) | async-done | bytes 32784 | tf_op jit(solution)/shard_map/reduce_scatter | solution.py:61
  345.4 96.6 %reduce-scatter.3.cloned.1.call-done = f32[64,128]{1,0:T(8,128)} async-done(((f32[1024,128]{1,0:T(8,128)}), f32[64,128]{1,0:T(8,128)}) %reduce-scatter.3.cloned.1.call-update) | async-done | bytes 32784 | tf_op jit(solution)/shard_map/reduce_scatter | solution.py:62
  442.0 1.4 fusion.14
  443.4 42.6 %all_gather.24 = f32[1024,128]{1,0:T(8,128)S(1)} all-gather(f32[64,128]{1,0:T(8,128)S(1)} %get-tuple-element.7), channel_id=1, replica_groups=mesh['rx'=32,'tx'=16] {'tx'}, dimensions={0}, use_global_device_ids=true | all-gather | bytes 557056 | tf_op jit(solution)/shard_map/all_gather | solution.py:66
  486.0 64.4 %all_gather.25 = f32[1024,128]{1,0:T(8,128)S(1)} all-gather(f32[64,128]{1,0:T(8,128)S(1)} %get-tuple-element.6), channel_id=1, replica_groups=mesh['rx'=32,'tx'=16] {'tx'}, dimensions={0}, use_global_device_ids=true | all-gather | bytes 557056 | tf_op jit(solution)/shard_map/all_gather | solution.py:67
  550.4 0.1 broadcast_in_dim.7
  550.5 0.2 multiply_dynamic-update-slice_fusion
  550.7 16.2 %fusion.9 = f32[2048,128]{1,0:T(8,128)} fusion(f32[2048,128]{1,0:T(8,128)S(1)} %multiply_dynamic-update-slice_fusion, f32[1024,128]{1,0:T(8,128)S(1)} %all_gather.25, f32[2048]{0:T(1024)S(1)} %bitcast.29, f32[1024]{0:T(1024)S(1)} %bitcast.35, f32[2048]{0:T(1024)S(1)} %bitcast.26, f32[1024]{0:T(1024)S(1)} %bitcast.32, s32[2048]{0:T(1024)S(1)} %iota_add_fusion, ...), kind=kOutput, calls=%fused_computation.12 | convolution fusion | flops 3240361984 | bytes 2658304 | tf_op jit(solution)/shard_map/dot_general | solution.py:73
  567.0 0.0 all-gather.8.cloned.1.call-update
  567.6 367.2 %all-gather.8.cloned.1.call-done = f32[65536,128]{1,0:T(8,128)} async-done(((f32[2048,128]{1,0:T(8,128)}), f32[65536,128]{1,0:T(8,128)}) %all-gather.8.cloned.1.call-update) | async-done | bytes 33554448 | tf_op jit(solution)/shard_map/all_gather | solution.py:33
  934.9 0.0 copy-start
  934.9 11.7 %reduce_sum.28 = f32[2048,128]{1,0:T(8,128)S(1)} reduce(f32[32,2048,128]{2,1,0:T(8,128)} %bitcast.21, f32[]{:T(128)} %constant.38.clone.1), dimensions={0}, to_apply=%region_3.4 | reduce | flops 8126464 | bytes 34603012 | tf_op jit(solution)/shard_map/reduce_sum | solution.py:34
  946.6 0.0 copy-done
  946.6 0.6 subtract_reduce_fusion
  947.2 0.0 copy-start.2
  947.2 100.9 %psum.7 = f32[]{:T(128)} all-reduce(f32[]{:T(128)} %get-tuple-element.4), channel_id=1, replica_groups=mesh['rx'=32,'tx'=16] {'rx','tx'}, use_global_device_ids=true, to_apply=%region_5.6 | all-reduce | flops 1 | bytes 8 | tf_op jit(solution)/shard_map/psum | solution.py:82
  1048.1 0.6 multiply_add_fusion
  1049.4 0.0 copy-done.2
  (8 shorter events, 0.0 us)
Async XLA Ops:
  7.2 209.6 %all-gather.6.cloned.1.call-start = ((), (), s32[]{:S(2)}) async-start(), calls=%async_computation.2 | async-start | bytes 1081344 | tf_op jit(solution)/shard_map/all_gather | solution.py:42
  7.9 337.5 %reduce-scatter.5.cloned.1.call-start = ((), (), s32[]{:S(2)}) async-start(), calls=%async_computation.4 | async-start | bytes 557056 | tf_op jit(solution)/shard_map/reduce_scatter | solution.py:61
  216.7 13.8 %copy-start.1 = (f32[2048,128]{1,0:T(8,128)S(1)}, f32[2048,128]{1,0:T(8,128)}, u32[]{:S(2)}) copy-start(f32[2048,128]{1,0:T(8,128)} %all-gather.6.cloned.1.call-done) | copy-start | bytes 3145732
  216.7 14.9 %copy-start.3 = (s32[64]{0:T(128)S(1)}, s32[64]{0:T(128)}, u32[]{:S(2)}) copy-start(s32[64]{0:T(128)} %param.10) | copy-start | bytes 772
  216.7 14.9 %copy-start.4 = (s32[64]{0:T(128)S(1)}, s32[64]{0:T(128)}, u32[]{:S(2)}) copy-start(s32[64]{0:T(128)} %param.9) | copy-start | bytes 772
  227.4 214.6 %reduce-scatter.3.cloned.1.call-start = ((), (), s32[]{:S(2)}) async-start(), calls=%async_computation.3 | async-start | bytes 557056 | tf_op jit(solution)/shard_map/reduce_scatter | solution.py:62
  231.6 703.3 %all-gather.8.cloned.1.call-start = ((), (), s32[]{:S(2)}) async-start(), calls=%async_computation.5 | async-start | bytes 34603008 | tf_op jit(solution)/shard_map/all_gather | solution.py:33
  934.9 11.7 %copy-start = (f32[64,128]{1,0:T(8,128)S(1)}, f32[64,128]{1,0:T(8,128)}, u32[]{:S(2)}) copy-start(f32[64,128]{1,0:T(8,128)} %param.8) | copy-start | bytes 98308
  947.2 102.2 %copy-start.2 = (f32[64,128]{1,0:T(8,128)}, f32[64,128]{1,0:T(8,128)S(1)}, u32[]{:S(2)}) copy-start(f32[64,128]{1,0:T(8,128)S(1)} %get-tuple-element.5) | copy-start | bytes 98308
Sparse Core Ops, SparseCore 0:
  10.1 206.6 all-gather.5
  227.5 117.8 reduce-scatter.4
  350.8 91.2 reduce-scatter.2
  567.1 367.7 all-gather.7
